TPU v7x, 32 devices: a whole 2x2x4 slice. The times are simulated.
32 devices in a mesh: groups: 2 (over x), heads: 16 (over z, y, core).
Axes of the slice: x: 2, y: 2, z: 4, core: 2. Of those that a mesh axis runs over, the one named last changes fastest.
Arguments:
- prompt_hidden: bfloat16 [8192, 7168], P(('groups', 'heads')), parts along dimension 0, may hold values from -6 to 6
- prompt_len: int32 [4], P('groups'), parts along dimension 0, may hold values from 1 to 2048, 2560 in all
- owners: int32 [4], P('groups'), parts along dimension 0, may hold values from 0 to 15
- down_weight: bfloat16 [7168, 576], P('heads'), may hold values from -0.0625 to 0.0625
- latent_gain: float32 [512], replicated, may hold values from 0.5 to 1.5
- decode_hidden: bfloat16 [16, 7168], P('groups'), parts along dimension 0, may hold values from -6 to 6
- context_len: int32 [16], P('groups'), parts along dimension 0, may hold values from 256 to 1024, as said below
- query_nope: bfloat16 [16, 16, 128], P('groups', 'heads'), parts along dimension 0, may hold values from -6 to 6
- query_rope: bfloat16 [16, 16, 64], P('groups', 'heads'), parts along dimension 0, may hold values from -8 to 8
- key_absorb: bfloat16 [16, 128, 512], P('heads'), may hold values from -0.5 to 0.5
- value_absorb: bfloat16 [16, 512, 128], P('heads'), may hold values from -0.25 to 0.25
- out_weight: bfloat16 [2048, 7168], P('heads'), may hold values from -0.1875 to 0.1875
- cache: bfloat16 [16, 1024, 576], P('groups', 'heads'), parts along dimension 0, may hold values from -8 to 8
Outputs:
- new_cache: bfloat16 [4, 2048, 576], P('groups', 'heads'), parts along dimension 0
- attn_out: bfloat16 [16, 7168], P('groups'), parts along dimension 0
There are 2 independent parts, one for each index of `groups`. A program takes and returns all parts, laid end to end along the dimension named above; an argument that names none is the same for every part. Nothing has to cross between parts.
Inputs may be any that keep to these rules, and one draw needn't show every extreme that they name: `prompt_len`: within each part (each index of groups) they sum to 2560. `context_len`: within each part some request has exactly 1024.
All inputs are finite; a program needn't handle non-finite values.
Results may differ from a plain program's by a relative error of at most 0.008.
Values may be sent and summed in bfloat16 or wider, within the bound.
A program may use at most 64 MiB of HBM per device.

v0:
```python
import math

import jax
import jax.numpy as jnp
from jax import lax
from jax.sharding import PartitionSpec as P

PSPLIT = 8


def latent_rows(kv_rows, positions, gain_vec):
    row_width = gain_vec.shape[0]
    latent = kv_rows[..., :row_width]
    rotary = kv_rows[..., row_width:]
    latent = (
        latent * lax.rsqrt(jnp.mean(latent * latent, axis=-1, keepdims=True) + 1e-06) * gain_vec
    )
    half_rope = rotary.shape[-1] // 2
    frequency = jnp.exp(jnp.arange(half_rope, dtype=jnp.float32) * (-math.log(10000.0) / half_rope))
    angles = positions.astype(jnp.float32)[..., None] * frequency
    cosine = jnp.cos(angles)
    sine_part = jnp.sin(angles)
    leading = rotary[..., :half_rope]
    second = rotary[..., half_rope:]
    turned = jnp.concatenate(
        [leading * cosine - second * sine_part, second * cosine + leading * sine_part], axis=-1
    )
    return jnp.concatenate([latent, turned], axis=-1)


def local(
    prompt_hidden,
    prompt_len,
    owners,
    down_weight,
    latent_gain,
    decode_hidden,
    context_len,
    query_nope,
    query_rope,
    key_absorb,
    value_absorb,
    out_weight,
    cache,
):
    members = lax.axis_size("heads")
    device = lax.axis_index("heads")
    rows_here, model_width = prompt_hidden.shape
    row_width = down_weight.shape[1]
    lat_width = latent_gain.shape[0]
    shard_rows = lax.all_gather(down_weight, "heads", axis=0, tiled=True)
    kv_new = jnp.dot(prompt_hidden, shard_rows, preferred_element_type=jnp.float32)
    kv_dec = jnp.dot(decode_hidden, shard_rows, preferred_element_type=jnp.float32)
    prompt_slot = device // PSPLIT
    length_here = lax.dynamic_index_in_dim(prompt_len, prompt_slot, 0, keepdims=False)
    owner_here = lax.dynamic_index_in_dim(owners, prompt_slot, 0, keepdims=False)
    start_row = device % PSPLIT * rows_here
    positions = start_row + jnp.arange(rows_here, dtype=jnp.int32)
    entries = latent_rows(kv_new, positions, latent_gain)
    entries = jnp.where((positions < length_here)[:, None], entries, 0.0).astype(jnp.bfloat16)
    layout = entries.reshape(rows_here // members, members, row_width)
    rotated = jnp.roll(layout, owner_here, axis=1)
    outgoing = rotated.transpose(1, 0, 2)
    arrived = lax.all_to_all(outgoing, "heads", split_axis=0, concat_axis=0, tiled=True)
    new_cache = arrived.reshape(members // PSPLIT, PSPLIT * (rows_here // members), row_width)
    own_keys = latent_rows(kv_dec, context_len, latent_gain).astype(jnp.bfloat16)
    own_latent = own_keys[:, :lat_width].astype(jnp.float32)
    query_latent = jnp.dot(
        query_nope[:, 0], key_absorb[0], preferred_element_type=jnp.float32
    ).astype(jnp.bfloat16)
    query_own = jnp.concatenate([query_latent, query_rope[:, 0]], axis=-1)
    query_all = lax.all_gather(query_own[:, None], "heads", axis=1, tiled=True)
    score_scale = 1.0 / math.sqrt(query_nope.shape[-1] + query_rope.shape[-1])
    position = jnp.arange(cache.shape[1], dtype=jnp.int32) * members + device
    is_live = (position[None, :] < context_len[:, None])[:, None, :]
    scores = (
        jnp.einsum("rhk,rik->rhi", query_all, cache, preferred_element_type=jnp.float32)
        * score_scale
    )
    scores = jnp.where(is_live, scores, -1e30)
    block_max = jnp.max(scores, axis=-1)
    weights = jnp.where(is_live, jnp.exp(scores - block_max[..., None]), 0.0)
    block_total = jnp.sum(weights, axis=-1)
    partial_value = jnp.einsum(
        "rhi,ril->rhl",
        weights.astype(jnp.bfloat16),
        cache[..., :lat_width],
        preferred_element_type=jnp.float32,
    )
    got_partial, got_max, got_total = (
        lax.all_to_all(partial_value[None], "heads", split_axis=2, concat_axis=0, tiled=True),
        lax.all_to_all(block_max[None], "heads", split_axis=2, concat_axis=0, tiled=True),
        lax.all_to_all(block_total[None], "heads", split_axis=2, concat_axis=0, tiled=True),
    )
    got_partial = got_partial[:, :, 0]
    got_max = got_max[:, :, 0]
    got_total = got_total[:, :, 0]
    own_score = (
        jnp.sum(query_own.astype(jnp.float32) * own_keys.astype(jnp.float32), axis=-1) * score_scale
    )
    ceiling = jnp.maximum(jnp.max(got_max, axis=0), own_score)
    factor = jnp.exp(got_max - ceiling[None])
    gathered = jnp.sum(factor[..., None] * got_partial, axis=0)
    summed = jnp.sum(factor * got_total, axis=0)
    own_weight = jnp.exp(own_score - ceiling)
    summed = summed + own_weight
    gathered = gathered + own_weight[:, None] * own_latent
    latent_out = (gathered / summed[:, None]).astype(jnp.bfloat16)
    head_out = jnp.dot(latent_out, value_absorb[0], preferred_element_type=jnp.float32).astype(
        jnp.bfloat16
    )
    head_term = jnp.dot(head_out, out_weight, preferred_element_type=jnp.float32)
    attn_out = lax.psum(head_term, "heads").astype(jnp.bfloat16)
    return (new_cache, attn_out)


def solution(mesh):
    placed = (
        P(("groups", "heads"), None),
        P("groups"),
        P("groups"),
        P("heads", None),
        P(),
        P("groups", None),
        P("groups"),
        P("groups", "heads", None),
        P("groups", "heads", None),
        P("heads", None, None),
        P("heads", None, None),
        P("heads", None),
        P("groups", "heads", None),
    )
    return jax.shard_map(
        local,
        mesh=mesh,
        in_specs=placed,
        out_specs=(P("groups", "heads", None), P("groups", None)),
        check_vma=False,
    )
```

profile of v0, /device:TPU:0, one launch (start us, length us, event | category | flops | bytes accessed | tf_op | source)
XLA Modules:
  0.0 187.4 jit_solution(16863117908616133937)
XLA Ops:
  7.2 0.0 all-gather.4.cloned.1.call-start
  7.3 0.7 all-gather.4.cloned.1.call-update
  8.0 1.0 convolution_convert_fusion
  9.0 0.7 fusion.26
  9.7 24.1 %all-gather.1 = bf16[16,576,8]{1,2,0:T(8,128)(2,1)S(1)} all-gather(bf16[1,576,8]{1,2,0:T(8,128)(2,1)S(1)} %fusion.26), channel_id=2, replica_groups=mesh['groups'=2,'heads'=16] {'heads'}, dimensions={0}, use_global_device_ids=true | all-gather | bytes 156672 | tf_op jit(solution)/shard_map/all_gather | solution.py:72
  33.8 0.2 reshape.121
  34.0 0.2 reshape.119
  34.2 0.7 broadcast_compare_fusion
  34.9 1.5 fusion.41
  36.4 0.7 copy.26
  37.1 3.5 %all-to-all-start.1 = ((f32[1,8,16]{1,0,2:T(1,128)}), f32[1,8,16]{1,0,2:T(1,128)S(1)}, u32[]{:S(2)}, u32[]{:S(2)}) async-start(f32[1,8,16]{1,0,2:T(1,128)} %copy.26), calls=%async_computation.1 | async-start | bytes 16384 | tf_op jit(solution)/shard_map/all_to_all | solution.py:92
  40.6 1.2 dynamic_slice.11
  41.8 0.7 add_compare_fusion
  42.5 0.2 fusion.10
  42.7 1.3 convolution_bitcast_fusion
  44.0 0.6 dynamic_slice.12
  45.7 0.7 copy.30
  47.0 6.0 %all-to-all-start.3 = ((f32[1,8,16]{1,0,2:T(1,128)}), f32[1,8,16]{1,0,2:T(1,128)S(1)}, u32[]{:S(2)}, u32[]{:S(2)}) async-start(f32[1,8,16]{1,0,2:T(1,128)} %copy.30), calls=%async_computation.3 | async-start | bytes 16384 | tf_op jit(solution)/shard_map/all_to_all | solution.py:93
  53.0 0.9 copy.29
  53.9 0.1 copy.27
  54.0 5.5 %all-to-all-done.3 = f32[1,8,16]{1,0,2:T(1,128)S(1)} async-done(((f32[1,8,16]{1,0,2:T(1,128)}), f32[1,8,16]{1,0,2:T(1,128)S(1)}, u32[]{:S(2)}, u32[]{:S(2)}) %all-to-all-start.3) | async-done | bytes 544 | tf_op jit(solution)/shard_map/all_to_all | solution.py:93
  59.5 3.5 %all-to-all-start.2 = ((f32[1,8,16,512]{3,1,0,2:T(8,128)}), f32[1,8,16,512]{3,1,0,2:T(8,128)S(1)}, u32[]{:S(2)}, u32[]{:S(2)}) async-start(f32[1,8,16,512]{3,1,0,2:T(8,128)} %copy.29), calls=%async_computation.2 | async-start | bytes 524288 | tf_op jit(solution)/shard_map/all_to_all | solution.py:91
  63.0 0.1 copy.31
  63.1 33.4 %all-gather.4.cloned.1.call-done = bf16[7168,576]{1,0:T(8,128)(2,1)} async-done(((bf16[448,576]{1,0:T(8,128)(2,1)}), bf16[7168,576]{1,0:T(8,128)(2,1)}) %all-gather.4.cloned.1.call-update) | async-done | bytes 8257552 | tf_op jit(solution)/shard_map/all_gather | solution.py:51
  96.5 5.0 %fusion.43 = f32[8,576]{1,0:T(8,128)S(1)} fusion(bf16[8,7168]{1,0:T(8,128)(2,1)S(1)} %copy-done.2, bf16[7168,576]{1,0:T(8,128)(2,1)} %all-gather.4.cloned.1.call-done), kind=kOutput, calls=%fused_computation.69 | convolution fusion | flops 66060288 | bytes 8390656 | tf_op jit(solution)/shard_map/dot_general | solution.py:53
  101.5 0.1 multiply_reduce_fusion.2
  101.7 1.0 copy-done.1
  102.7 1.0 copy-done.7
  103.8 3.7 %fusion.42 = f32[256,576]{0,1:T(8,128)S(1)} fusion(bf16[256,7168]{1,0:T(8,128)(2,1)S(1)} %copy-done.7, bf16[7168,576]{1,0:T(8,128)(2,1)S(1)} %copy-done.1), kind=kOutput, calls=%fused_computation.68 | convolution fusion | flops 2113929216 | bytes 12517376 | tf_op jit(solution)/shard_map/dot_general | solution.py:52
  107.5 0.1 multiply_reduce_fusion
  107.6 0.1 fusion.32
  107.7 0.2 fusion.16
  107.9 0.1 multiply_convert_fusion
  108.0 0.1 multiply_multiply_fusion
  108.1 0.1 copy.21
  108.3 0.1 copy.22
  108.4 0.1 copy.23
  108.5 0.2 fusion.2
  108.7 0.3 fusion.5
  108.9 0.8 copy.24
  109.7 0.2 multiply_reduce_fusion.1
  109.9 0.2 fusion.35
  110.1 3.9 %all-to-all-start = ((bf16[16,16,576]{2,1,0:T(8,128)(2,1)}), bf16[16,16,576]{2,1,0:T(8,128)(2,1)S(1)}, u32[]{:S(2)}, u32[]{:S(2)}) async-start(bf16[16,16,576]{2,1,0:T(8,128)(2,1)} %copy.24), calls=%async_computation | async-start | bytes 655360 | tf_op jit(solution)/shard_map/all_to_all | solution.py:64
  114.0 0.1 copy.28
  114.1 0.1 fusion.6
  114.2 0.5 fusion.1
  114.7 64.9 %all-reduce.1 = bf16[8,7168]{1,0:T(8,128)(2,1)} all-reduce(f32[8,7168]{1,0:T(8,128)S(1)} %fusion.1), channel_id=1, replica_groups=mesh['groups'=2,'heads'=16] {'heads'}, use_global_device_ids=true, to_apply=%region_8.9 | all-reduce | flops 57344 | bytes 344064 | tf_op jit(solution)/shard_map/psum | solution.py:113
  179.6 0.9 copy.32
  (29 shorter events, 0.2 us)
Async XLA Ops:
  7.2 107.0 %copy-start = (bf16[128,7168]{1,0:T(8,128)(2,1)S(1)}, bf16[128,7168]{1,0:T(8,128)(2,1)}, u32[]{:S(2)}) copy-start(bf16[128,7168]{1,0:T(8,128)(2,1)} %param.24) | copy-start | bytes 5505028
  7.2 45.8 %copy-start.6 = (s32[8]{0:T(128)S(1)}, s32[8]{0:T(128)}, u32[]{:S(2)}) copy-start(s32[8]{0:T(128)} %param.19) | copy-start | bytes 100
  7.2 36.8 %copy-start.8 = (s32[2]{0:T(128)S(1)}, s32[2]{0:T(128)}, u32[]{:S(2)}) copy-start(s32[2]{0:T(128)} %param.15) | copy-start | bytes 28
  7.2 89.3 %copy-start.2 = (bf16[8,7168]{1,0:T(8,128)(2,1)S(1)}, bf16[8,7168]{1,0:T(8,128)(2,1)}, u32[]{:S(2)}) copy-start(bf16[8,7168]{1,0:T(8,128)(2,1)} %param.18) | copy-start | bytes 344068
  7.2 89.3 %all-gather.4.cloned.1.call-start = ((), (), s32[]{:S(2)}) async-start(), calls=%async_computation.4 | async-start | bytes 9748480 | tf_op jit(solution)/shard_map/all_gather | solution.py:51
  37.1 9.9 %all-to-all-start.1 = ((f32[1,8,16]{1,0,2:T(1,128)}), f32[1,8,16]{1,0,2:T(1,128)S(1)}, u32[]{:S(2)}, u32[]{:S(2)}) async-start(f32[1,8,16]{1,0,2:T(1,128)} %copy.26), calls=%async_computation.1 | async-start | bytes 16384 | tf_op jit(solution)/shard_map/all_to_all | solution.py:92
  47.0 12.4 %all-to-all-start.3 = ((f32[1,8,16]{1,0,2:T(1,128)}), f32[1,8,16]{1,0,2:T(1,128)S(1)}, u32[]{:S(2)}, u32[]{:S(2)}) async-start(f32[1,8,16]{1,0,2:T(1,128)} %copy.30), calls=%async_computation.3 | async-start | bytes 16384 | tf_op jit(solution)/shard_map/all_to_all | solution.py:93
  59.5 50.6 %all-to-all-start.2 = ((f32[1,8,16,512]{3,1,0,2:T(8,128)}), f32[1,8,16,512]{3,1,0,2:T(8,128)S(1)}, u32[]{:S(2)}, u32[]{:S(2)}) async-start(f32[1,8,16,512]{3,1,0,2:T(8,128)} %copy.29), calls=%async_computation.2 | async-start | bytes 524288 | tf_op jit(solution)/shard_map/all_to_all | solution.py:91
  96.5 6.2 %copy-start.1 = (bf16[7168,576]{1,0:T(8,128)(2,1)S(1)}, bf16[7168,576]{1,0:T(8,128)(2,1)}, u32[]{:S(2)}) copy-start(bf16[7168,576]{1,0:T(8,128)(2,1)} %all-gather.4.cloned.1.call-done) | copy-start | bytes 24772612
  96.5 7.3 %copy-start.7 = (bf16[256,7168]{1,0:T(8,128)(2,1)S(1)}, bf16[256,7168]{1,0:T(8,128)(2,1)}, u32[]{:S(2)}) copy-start(bf16[256,7168]{1,0:T(8,128)(2,1)} %param.13) | copy-start | bytes 11010052
  103.8 4.1 %copy-start.4 = (f32[512]{0:T(512)S(1)}, f32[512]{0:T(512)}, u32[]{:S(2)}) copy-start(f32[512]{0:T(512)} %param.17) | copy-start | bytes 6148
  107.5 2.2 %copy-start.5 = (bf16[8,1,64]{2,0,1:T(8,128)(2,1)S(1)}, bf16[8,1,64]{2,0,1:T(8,128)(2,1)}, u32[]{:S(2)}) copy-start(bf16[8,1,64]{2,0,1:T(8,128)(2,1)} %param.21) | copy-start | bytes 3076
  107.5 6.7 %copy-start.3 = (bf16[1,512,128]{2,1,0:T(8,128)(2,1)S(1)}, bf16[1,512,128]{2,1,0:T(8,128)(2,1)}, u32[]{:S(2)}) copy-start(bf16[1,512,128]{2,1,0:T(8,128)(2,1)} %param.23) | copy-start | bytes 393220
  110.1 69.5 %all-to-all-start = ((bf16[16,16,576]{2,1,0:T(8,128)(2,1)}), bf16[16,16,576]{2,1,0:T(8,128)(2,1)S(1)}, u32[]{:S(2)}, u32[]{:S(2)}) async-start(bf16[16,16,576]{2,1,0:T(8,128)(2,1)} %copy.24), calls=%async_computation | async-start | bytes 655360 | tf_op jit(solution)/shard_map/all_to_all | solution.py:64
Sparse Core Ops, SparseCore 0:
  10.3 86.1 all-gather.3
where the time goes:
time: 188 us; the launch traced here: 187 us
  blocking collectives  89 us (47%)
  waiting for transfers between devices  39.6 us (21%)
  starting transfers between devices  16.9 us (9%)
  between operations  16.1 us (9%)
  matrix products  13.1 us (7%)
  local copies, waits for them, and re-layouts  8.78 us (5%)
  other arithmetic  3.93 us (2%)
    psum x1, blocking collectives, local(): attn_out = lax.psum(head_term, 'heads').astype(jnp.bfloat16)  64.9 us
    all_gather x1, waiting for transfers between devices, local(): shard_rows = lax.all_gather(down_weight, 'heads', axis=0, tiled=True)  33.4 us
    all_gather x1, blocking collectives, local(): query_all = lax.all_gather(query_own[:, None], 'heads', axis=1, tiled=True)  24.1 us
    all_to_all x1, starting transfers between devices, local(): lax.all_to_all(block_total[None], 'heads', split_axis=2, concat_axis=0, t...  5.96 us
    all_to_all x1, waiting for transfers between devices, local(): lax.all_to_all(block_total[None], 'heads', split_axis=2, concat_axis=0, t...  5.47 us
    dot_general x1, matrix products, local(): jnp.dot(decode_hidden, shard_rows, preferred_element_type=jnp.float32)  5.04 us
    all_to_all x1, starting transfers between devices, local(): lax.all_to_all(outgoing, 'heads', split_axis=0, concat_axis=0, tiled=True)  3.91 us
  transfers between devices with their start and end apart: 5, of which 2 were waited for; matrix products, arithmetic and copies ran while one was open for 12% of the time, Pallas kernels for 0%

commit v1 on v0

--- a/solution.py
+++ b/solution.py
@@ -3,6 +3,8 @@
 import jax
 import jax.numpy as jnp
 from jax import lax
+from jax.experimental import pallas as pl
+from jax.experimental.pallas import tpu as pltpu
 from jax.sharding import PartitionSpec as P
 
 PSPLIT = 8
@@ -114,6 +116,399 @@
     return (new_cache, attn_out)
 
 
+MESH = pl.DeviceIdType.MESH
+RING_A = 144
+RING_C = 160
+
+
+def fused_body(
+    plen, own, clen, w_ref, gain_ref, dh_ref, qn_ref, qr_ref, ka_ref, va_ref, tab_ref, dtab_ref,
+    hid_hbm, ow_hbm, cache_hbm,
+    new_ref, attn_ref,
+    wbuf, hb, ow, cb, acc, qbuf, kvs, kvr, msg, got, hp, rs, agp, ag, ent,
+    loc, ring_s, core_s, x_s, in_r, core_r,
+    q_s, q_r, qc_s, qc_r, kv_s, kv_r, a_s, a_r, rs_s, rs_r, ag_s, ag_r, n_s, n_r,
+):
+    me = lax.axis_index("heads")
+    g = lax.axis_index("groups")
+    k = me // 2
+    c = me % 2
+    z = k // 2
+    y = k % 2
+    pos = y * (7 - 2 * z) + z
+    rows = w_ref.shape[0]
+    width = w_ref.shape[1]
+    lat = gain_ref.shape[1]
+    scale = 1.0 / math.sqrt(qn_ref.shape[1] + qr_ref.shape[1])
+    f32, bf16 = jnp.float32, jnp.bfloat16
+
+    def chip(p):
+        q = (p + 16) % 8
+        hi = q // 4
+        return hi * (15 - 2 * q) + (1 - hi) * 2 * q
+
+    def heads(d):
+        return {"heads": d}
+
+    sib = me + 1 - 2 * c
+    right = chip(pos + 1) * 2 + c
+    left = chip(pos - 1) * 2 + c
+
+    local_copies = [
+        pltpu.make_async_copy(hid_hbm, hb, loc.at[0]),
+        pltpu.make_async_copy(ow_hbm, ow, loc.at[1]),
+        pltpu.make_async_copy(cache_hbm, cb, loc.at[2]),
+        pltpu.make_async_copy(w_ref, wbuf.at[k, pl.ds(pl.multiple_of(c * rows, 16), rows)], loc.at[3]),
+    ]
+    for cp in (local_copies[3], local_copies[2], local_copies[0], local_copies[1]):
+        cp.start()
+
+    barrier = pltpu.get_barrier_semaphore()
+
+    def greet(i, carry):
+        pl.semaphore_signal(barrier, inc=1, device_id=heads((me + i) % 16), device_id_type=MESH)
+        return carry
+
+    lax.fori_loop(1, 16, greet, 0)
+    pl.semaphore_signal(barrier, inc=1, device_id={"groups": 1 - g}, device_id_type=MESH)
+
+    starts = (304 * g, RING_A, 304 * (1 - g))
+    sizes = (RING_A, RING_C, RING_A)
+
+    def piece(kk, cc, role):
+        return wbuf.at[kk, pl.ds(pl.multiple_of(cc * rows + starts[role], 16), sizes[role])]
+
+    def w_piece(role):
+        return w_ref.at[pl.ds(pl.multiple_of(starts[role], 16), sizes[role])]
+
+    sends = []
+
+    def send(src, dst, ssem, rsem, dev):
+        cp = pltpu.make_async_remote_copy(
+            src_ref=src, dst_ref=dst, send_sem=ssem, recv_sem=rsem, device_id=dev, device_id_type=MESH
+        )
+        cp.start()
+        sends.append(cp)
+
+    def arrived(dst, rsem):
+        pltpu.make_async_copy(dst, dst, rsem).wait()
+
+    def q_copy(i):
+        dest = ((k + i) % 8) * 2 + c
+        return pltpu.make_async_remote_copy(
+            src_ref=qbuf.at[c, k], dst_ref=qbuf.at[c, k], send_sem=q_s.at[i], recv_sem=q_r.at[i],
+            device_id=heads(dest), device_id_type=MESH,
+        )
+
+    qlat = jnp.dot(qn_ref[...], ka_ref[...], preferred_element_type=f32).astype(bf16).astype(f32)
+    q_own = jnp.concatenate([qlat, qr_ref[...].astype(f32)], axis=-1)
+    qbuf[c, k] = q_own
+    wide = dh_ref[:, pl.ds(pl.multiple_of(k * 2 * rows, 128), 2 * rows)].astype(f32)
+    part = jnp.where(c == 0, wide[:, :rows], wide[:, rows:]).astype(bf16)
+    kvs[0] = jnp.dot(part, w_ref[...], preferred_element_type=f32)
+
+    pl.semaphore_wait(barrier, 16)
+
+    lax.fori_loop(1, 8, lambda i, t: (q_copy(i).start(), t)[1], 0)
+
+    def kv_send(step):
+        b = 1 << step
+        dest = me + b - 2 * b * ((me // b) % 2)
+        send(kvs.at[step], kvr.at[step], kv_s.at[step], kv_r.at[step], heads(dest))
+
+    def kv_take(step):
+        arrived(kvr.at[step], kv_r.at[step])
+        kvs[step + 1] = kvs[step] + kvr[step]
+
+    kv_send(0)
+    for role in range(2):
+        mine = piece(k, c, role)
+        send(w_piece(role), mine, ring_s.at[0, k, role], in_r.at[k, role], heads(right))
+        send(w_piece(role), mine, ring_s.at[1, k, role], in_r.at[k, role], heads(left))
+    for role in range(3):
+        send(w_piece(role), piece(k, c, role), core_s.at[k, role], core_r.at[k, role], heads(sib))
+
+    def to_core(kk, role):
+        p = piece(kk, c, role)
+        send(p, p, core_s.at[kk, role], core_r.at[kk, role], heads(sib))
+
+    def ring(s, role):
+        for way in range(2):
+            if s == 4 and role != way:
+                continue
+            kk = chip(pos - s) if way == 0 else chip(pos + s)
+            p = piece(kk, c, role)
+            arrived(p, in_r.at[kk, role])
+            if s < 3 or (s == 3 and role == way):
+                send(p, p, ring_s.at[way, kk, role], in_r.at[kk, role], heads(right if way == 0 else left))
+            if role == 0:
+                send(p, p, x_s.at[kk], in_r.at[kk, 2], {"groups": 1 - g})
+            to_core(kk, role)
+
+    def cross(s):
+        for kk in (chip(pos - s), chip(pos + s)) if s < 4 else (chip(pos + 4),):
+            arrived(piece(kk, c, 2), in_r.at[kk, 2])
+            to_core(kk, 2)
+
+    def matmul(kk, first=False):
+        for role in range(3):
+            arrived(piece(kk, 1 - c, role), core_r.at[kk, role])
+        h = hb[:, pl.ds(pl.multiple_of(kk * 2 * rows, 128), 2 * rows)]
+        v = jnp.dot(h, wbuf[kk], preferred_element_type=f32)
+        acc[...] = v if first else acc[...] + v
+
+    def finish(kv, table):
+        a = kv[:, :lat]
+        b = kv[:, lat:]
+        half = b.shape[1] // 2
+        a = a * lax.rsqrt(jnp.mean(a * a, axis=-1, keepdims=True) + 1e-06) * gain_ref[...]
+        turned = jnp.concatenate([b[:, half:], b[:, :half]], axis=-1)
+        b = b * table[:, : 2 * half] + turned * table[:, 2 * half :]
+        return jnp.concatenate([a, b], axis=-1)
+
+    lax.fori_loop(1, 8, lambda i, t: (q_copy(i).wait_recv(), t)[1], 0)
+    send(qbuf.at[c], qbuf.at[c], qc_s, qc_r, heads(sib))
+    kv_take(0)
+    kv_send(1)
+    local_copies[2].wait()
+    arrived(qbuf.at[1 - c], qc_r)
+
+    n_req = cb.shape[0]
+    per = cb.shape[1]
+    cols = n_req * per
+    q_all = qbuf[...].reshape(16 * n_req, width).astype(bf16)
+    cache = cb[...].reshape(cols, width)
+    scores = lax.dot_general(q_all, cache, (((1,), (1,)), ((), ())), preferred_element_type=f32) * scale
+    row_i = lax.broadcasted_iota(jnp.int32, scores.shape, 0)
+    col_i = lax.broadcasted_iota(jnp.int32, scores.shape, 1)
+    limit = jnp.zeros(scores.shape, jnp.int32)
+    for r in range(n_req):
+        limit = jnp.where(row_i % n_req == r, clen[r], limit)
+    live = (col_i // per == row_i % n_req) & ((col_i % per) * 16 + me < limit)
+    scores = jnp.where(live, scores, -1e30)
+    top = jnp.max(scores, axis=-1, keepdims=True)
+    wts = jnp.where(live, jnp.exp(scores - top), 0.0)
+    tot = jnp.sum(wts, axis=-1, keepdims=True)
+    pv = jnp.dot(wts.astype(bf16), cache[:, :lat], preferred_element_type=f32)
+    lane = lax.broadcasted_iota(jnp.int32, (16 * n_req, 128), 1)
+    stat = jnp.where(lane == 0, top, jnp.where(lane == 1, tot, 0.0))
+    msg[...] = jnp.concatenate([pv, stat], axis=-1).reshape(2, 8, n_req, lat + 128)
+
+    def a_copy(i):
+        dest = (me + i) % 16
+        return pltpu.make_async_remote_copy(
+            src_ref=msg.at[dest % 2, dest // 2], dst_ref=got.at[me], send_sem=a_s.at[i], recv_sem=a_r.at[i],
+            device_id=heads(dest), device_id_type=MESH,
+        )
+
+    lax.fori_loop(1, 16, lambda i, t: (a_copy(i).start(), t)[1], 0)
+    got[me] = msg[c, k]
+
+    ring(1, 0)
+    kv_take(1)
+    kv_send(2)
+    ring(1, 1)
+    kv_take(2)
+    kv_send(3)
+    ring(2, 0)
+    kv_take(3)
+    own_key = finish(kvs[4], dtab_ref[...]).astype(bf16).astype(f32)
+    own_score = jnp.sum(q_own * own_key, axis=-1, keepdims=True) * scale
+
+    def from_a(i, t):
+        arrived(got.at[(me + 16 - i) % 16], a_r.at[i])
+        return t
+
+    lax.fori_loop(1, 16, from_a, 0)
+    gmax = got[:, :, lat : lat + 1]
+    gtot = got[:, :, lat + 1 : lat + 2]
+    ceiling = jnp.maximum(jnp.max(gmax, axis=0), own_score)
+    fac = jnp.exp(gmax - ceiling[None])
+    own_w = jnp.exp(own_score - ceiling)
+    summed = jnp.sum(fac * gtot, axis=0) + own_w
+    gath = jnp.sum(fac * got[:, :, :lat], axis=0) + own_w * own_key[:, :lat]
+    lat_out = (gath / summed).astype(bf16)
+    head_out = jnp.dot(lat_out, va_ref[...], preferred_element_type=f32).astype(bf16)
+    local_copies[1].wait()
+    hp[...] = jnp.dot(head_out, ow[...], preferred_element_type=f32)
+
+    def span(d):
+        return pl.ds(pl.multiple_of((d // 2) * 896 + (d % 2) * 384, 128), 512)
+
+    def rs_copy(i):
+        dest = (me + i) % 16
+        return pltpu.make_async_remote_copy(
+            src_ref=hp.at[:, span(dest)], dst_ref=rs.at[me], send_sem=rs_s.at[i], recv_sem=rs_r.at[i],
+            device_id=heads(dest), device_id_type=MESH,
+        )
+
+    lax.fori_loop(1, 16, lambda i, t: (rs_copy(i).start(), t)[1], 0)
+    rs[me] = hp[:, span(me)]
+    ring(2, 1)
+    cross(1)
+
+    def from_rs(i, t):
+        arrived(rs.at[(me + 16 - i) % 16], rs_r.at[i])
+        return t
+
+    lax.fori_loop(1, 16, from_rs, 0)
+    total = jnp.sum(rs[...], axis=0)
+    packed = jnp.concatenate([total[:, :256], total[:, 256:]], axis=0).astype(bf16)
+    agp[...] = packed
+    ag[me] = packed
+
+    def ag_copy(i):
+        dest = (me + i) % 16
+        return pltpu.make_async_remote_copy(
+            src_ref=agp, dst_ref=ag.at[me], send_sem=ag_s.at[i], recv_sem=ag_r.at[i],
+            device_id=heads(dest), device_id_type=MESH,
+        )
+
+    lax.fori_loop(1, 16, lambda i, t: (ag_copy(i).start(), t)[1], 0)
+    ring(3, 0)
+    cross(2)
+    local_copies[0].wait()
+    local_copies[3].wait()
+    matmul(k, True)
+    ring(3, 1)
+    matmul(chip(pos - 1))
+    matmul(chip(pos + 1))
+
+    def from_ag(i, t):
+        arrived(ag.at[(me + 16 - i) % 16], ag_r.at[i])
+        return t
+
+    lax.fori_loop(1, 16, from_ag, 0)
+    for kk in range(8):
+        lo = ag[2 * kk].astype(f32)
+        hi = ag[2 * kk + 1].astype(f32)
+        attn_ref[:, kk * 896 : kk * 896 + 256] = lo[:8].astype(bf16)
+        attn_ref[:, kk * 896 + 256 : kk * 896 + 512] = lo[8:].astype(bf16)
+        attn_ref[:, kk * 896 + 512 : kk * 896 + 640] = hi[:8, 128:].astype(bf16)
+        attn_ref[:, kk * 896 + 640 : kk * 896 + 896] = hi[8:].astype(bf16)
+    matmul(chip(pos - 2))
+    matmul(chip(pos + 2))
+    ring(4, 0)
+    ring(4, 1)
+    cross(3)
+    matmul(chip(pos - 3))
+    matmul(chip(pos + 3))
+    cross(4)
+    matmul(chip(pos + 4))
+
+    slot = me // 8
+    m = hb.shape[0]
+    position = (me % 8) * m + lax.broadcasted_iota(jnp.int32, (m, 1), 0)
+    e = jnp.where(position < plen[slot], finish(acc[...], tab_ref[...]), 0.0).astype(bf16)
+    o_i = lax.broadcasted_iota(jnp.int32, (m, m), 0)
+    s_i = lax.broadcasted_iota(jnp.int32, (m, m), 1)
+    turn = (o_i // 16 - own[slot] + 16) % 16
+    perm = jnp.where(s_i == (o_i % 16) * 16 + turn, 1.0, 0.0).astype(bf16)
+    ent[...] = jnp.dot(perm, e, preferred_element_type=f32).astype(bf16).reshape(ent.shape)
+
+    def dst_of(src):
+        return new_ref.at[src // 8, pl.ds(pl.multiple_of((src % 8) * 16, 16), 16)]
+
+    def n_copy(i):
+        dest = (me + i) % 16
+        return pltpu.make_async_remote_copy(
+            src_ref=ent.at[dest], dst_ref=dst_of(me), send_sem=n_s.at[i], recv_sem=n_r.at[i],
+            device_id=heads(dest), device_id_type=MESH,
+        )
+
+    lax.fori_loop(1, 16, lambda i, t: (n_copy(i).start(), t)[1], 0)
+    new_ref[slot, pl.ds(pl.multiple_of((me % 8) * 16, 16), 16)] = ent[me]
+    for cp in sends:
+        cp.wait_send()
+    lax.fori_loop(1, 8, lambda i, t: (q_copy(i).wait_send(), t)[1], 0)
+
+    def drain(i, t):
+        a_copy(i).wait_send()
+        rs_copy(i).wait_send()
+        ag_copy(i).wait_send()
+        return t
+
+    lax.fori_loop(1, 16, drain, 0)
+
+    def from_n(i, t):
+        arrived(dst_of((me + 16 - i) % 16), n_r.at[i])
+        n_copy(i).wait_send()
+        return t
+
+    lax.fori_loop(1, 16, from_n, 0)
+
+
+def rope_table(positions, half):
+    frequency = jnp.exp(jnp.arange(half, dtype=jnp.float32) * (-math.log(10000.0) / half))
+    angles = positions.astype(jnp.float32)[:, None] * frequency
+    co, si = jnp.cos(angles), jnp.sin(angles)
+    return jnp.concatenate([co, co, -si, si], axis=-1)
+
+
+def fused(
+    prompt_hidden, prompt_len, owners, down_weight, latent_gain, decode_hidden, context_len,
+    query_nope, query_rope, key_absorb, value_absorb, out_weight, cache,
+):
+    device = lax.axis_index("heads")
+    m, model = prompt_hidden.shape
+    rows, width = down_weight.shape
+    lat = latent_gain.shape[0]
+    half = (width - lat) // 2
+    n_req = decode_hidden.shape[0]
+    per_prompt = 16 // prompt_len.shape[0]
+    positions = (device % per_prompt) * m + jnp.arange(m, dtype=jnp.int32)
+    table = rope_table(positions, half)
+    dtable = rope_table(context_len, half)
+    f32, bf16 = jnp.float32, jnp.bfloat16
+    vmem = pl.BlockSpec(memory_space=pltpu.VMEM)
+    smem = pl.BlockSpec(memory_space=pltpu.SMEM)
+    hbm = pl.BlockSpec(memory_space=pl.ANY)
+    dma = pltpu.SemaphoreType.DMA
+    return pl.pallas_call(
+        fused_body,
+        out_shape=(
+            jax.ShapeDtypeStruct((prompt_len.shape[0], m * per_prompt // 16, width), bf16),
+            jax.ShapeDtypeStruct((n_req, model), bf16),
+        ),
+        in_specs=[smem] * 3 + [vmem] * 9 + [hbm] * 3,
+        out_specs=(vmem, vmem),
+        scratch_shapes=[
+            pltpu.VMEM((8, 2 * rows, width), bf16),
+            pltpu.VMEM((m, model), bf16),
+            pltpu.VMEM(out_weight.shape, bf16),
+            pltpu.VMEM(cache.shape, bf16),
+            pltpu.VMEM((m, width), f32),
+            pltpu.VMEM((2, 8, n_req, width), f32),
+            pltpu.VMEM((5, n_req, width), f32),
+            pltpu.VMEM((4, n_req, width), f32),
+            pltpu.VMEM((2, 8, n_req, lat + 128), f32),
+            pltpu.VMEM((16, n_req, lat + 128), f32),
+            pltpu.VMEM((n_req, model), f32),
+            pltpu.VMEM((16, n_req, 512), f32),
+            pltpu.VMEM((16, 256), bf16),
+            pltpu.VMEM((16, 16, 256), bf16),
+            pltpu.VMEM((16, m // 16, width), bf16),
+            dma((4,)),
+            dma((2, 8, 2)),
+            dma((8, 3)),
+            dma((8,)),
+            dma((8, 3)),
+            dma((8, 3)),
+            dma((8,)), dma((8,)), dma, dma, dma((4,)), dma((4,)),
+            dma((16,)), dma((16,)), dma((16,)), dma((16,)), dma((16,)), dma((16,)), dma((16,)), dma((16,)),
+        ],
+        compiler_params=pltpu.CompilerParams(
+            collective_id=0, has_side_effects=True, vmem_limit_bytes=44 * 1024 * 1024
+        ),
+        cost_estimate=pl.CostEstimate(
+            flops=2 * m * model * width, bytes_accessed=2 * (m * model + model * width), transcendentals=0
+        ),
+    )(
+        prompt_len, owners, context_len, down_weight, latent_gain[None], decode_hidden, query_nope[:, 0],
+        query_rope[:, 0], key_absorb[0], value_absorb[0], table, dtable, prompt_hidden, out_weight, cache,
+    )
+
+
 def solution(mesh):
     placed = (
         P(("groups", "heads"), None),
@@ -130,8 +525,9 @@
         P("heads", None),
         P("groups", "heads", None),
     )
+    small = mesh.shape["heads"] == 16 and mesh.shape["groups"] == 2
     return jax.shard_map(
-        local,
+        fused if small else local,
         mesh=mesh,
         in_specs=placed,
         out_specs=(P("groups", "heads", None), P("groups", None)),

time: 188 us -> 90.4 us (0.48)
  the two profiles are of different devices: /device:TPU:0 before, /device:TPU:1 now
where the time goes in v1:
time: 90.4 us; the launch traced here: 89.3 us
  Pallas kernels  73.1 us (81%)
  local copies, waits for them, and re-layouts  13.9 us (15%)
  other arithmetic  1.57 us (2%)
    pallas_call x1, Pallas kernels, fused(): pl.pallas_call(fused_body, out_shape=(jax.ShapeDtypeStruct((prompt_len.sh...  73.1 us
    unnamed x27, local copies, waits for them, and re-layouts  13 us

profile of v1, /device:TPU:1, one launch (start us, length us, event | category | flops | bytes accessed | tf_op | source)
XLA Modules:
  0.0 89.3 jit_solution(16822022272013075393)
XLA Ops:
  0.7 0.7 convert_element_type.11
  1.3 0.1 multiply_cosine_fusion.1
  1.4 0.1 pad_maximum_fusion.1.dtab_ref
  1.5 0.5 multiply_cosine_fusion
  2.1 0.2 pad_maximum_fusion.tab_ref
  2.2 0.0 copy-start
  2.2 2.0 %copy-done = bf16[256,7168]{1,0:T(8,128)(2,1)S(1)} copy-done((bf16[256,7168]{1,0:T(8,128)(2,1)S(1)}, bf16[256,7168]{1,0:T(8,128)(2,1)}, u32[]{:S(2)}) %copy-start) | copy-done | bytes 3670040
  4.3 0.0 copy-start.1
  4.3 1.5 %copy-done.1 = bf16[128,7168]{1,0:T(8,128)(2,1)S(1)} copy-done((bf16[128,7168]{1,0:T(8,128)(2,1)S(1)}, bf16[128,7168]{1,0:T(8,128)(2,1)}, u32[]{:S(2)}) %copy-start.1) | copy-done | bytes 1835032
  5.8 0.0 copy-start.2
  5.8 1.1 %copy-done.2 = bf16[8,64,576]{2,1,0:T(8,128)(2,1)S(1)} copy-done((bf16[8,64,576]{2,1,0:T(8,128)(2,1)S(1)}, bf16[8,64,576]{2,1,0:T(8,128)(2,1)}, u32[]{:S(2)}) %copy-start.2) | copy-done | bytes 589848
  6.9 0.0 copy-start.3
  6.9 1.1 %copy-done.3 = bf16[448,576]{1,0:T(8,128)(2,1)S(1)} copy-done((bf16[448,576]{1,0:T(8,128)(2,1)S(1)}, bf16[448,576]{1,0:T(8,128)(2,1)}, u32[]{:S(2)}) %copy-start.3) | copy-done | bytes 516120
  7.9 0.0 copy-start.4
  7.9 0.9 %copy-done.4 = bf16[1,128,512]{2,1,0:T(8,128)(2,1)S(1)} copy-done((bf16[1,128,512]{2,1,0:T(8,128)(2,1)S(1)}, bf16[1,128,512]{2,1,0:T(8,128)(2,1)}, u32[]{:S(2)}) %copy-start.4) | copy-done | bytes 131096
  8.8 0.0 copy-start.5
  8.8 0.9 %copy-done.5 = bf16[1,512,128]{2,1,0:T(8,128)(2,1)S(1)} copy-done((bf16[1,512,128]{2,1,0:T(8,128)(2,1)S(1)}, bf16[1,512,128]{2,1,0:T(8,128)(2,1)}, u32[]{:S(2)}) %copy-start.5) | copy-done | bytes 131096
  9.7 0.0 copy-start.6
  9.7 0.9 %copy-done.6 = bf16[8,7168]{1,0:T(8,128)(2,1)S(1)} copy-done((bf16[8,7168]{1,0:T(8,128)(2,1)S(1)}, bf16[8,7168]{1,0:T(8,128)(2,1)}, u32[]{:S(2)}) %copy-start.6) | copy-done | bytes 114712
  10.6 0.0 copy-start.7
  10.6 0.7 copy-done.7
  11.3 0.0 copy-start.8
  11.3 0.7 copy-done.8
  12.0 0.0 copy-start.9
  12.0 0.7 copy-done.9
  12.7 0.0 copy-start.10
  12.7 0.7 copy-done.10
  13.3 0.0 copy-start.11
  13.3 0.7 copy-done.11
  14.0 0.0 copy-start.12
  14.0 0.7 copy-done.12
  14.6 73.1 %shard_map.140 = (bf16[2,128,576]{2,1,0:T(8,128)(2,1)S(1)}, bf16[8,7168]{1,0:T(8,128)(2,1)S(1)}) custom-call(s32[2]{0:T(128)S(1)} %copy-done.10, s32[2]{0:T(128)S(1)} %copy-done.11, s32[8]{0:T(128)S(1)} %copy-done.12, bf16[448,576]{1,0:T(8,128)(2,1)S(1)} %copy-done.3, f32[1,512]{1,0:T(1,128)S(1)} %bitcast.7, bf16[8,7168]{1,0:T(8,128)(2,1)S(1)} %copy-done.6, ...), custom_call_target="tpu_custom_call" | custom-call | flops 2113929216 | bytes 11927552 | tf_op jit(solution)/shard_map/pallas_call | solution.py:467
  87.8 0.9 %copy.17 = bf16[2,128,576]{1,2,0:T(8,128)(2,1)} copy(bf16[2,128,576]{2,1,0:T(8,128)(2,1)S(1)} %get-tuple-element.4) | data formatting | bytes 589824 | tf_op jit(solution)/shard_map/pallas_call | solution.py:467
  88.7 0.6 copy.19
  (2 shorter events, 0.0 us)
Async XLA Ops:
  2.2 2.0 %copy-start = (bf16[256,7168]{1,0:T(8,128)(2,1)S(1)}, bf16[256,7168]{1,0:T(8,128)(2,1)}, u32[]{:S(2)}) copy-start(bf16[256,7168]{1,0:T(8,128)(2,1)} %hid_hbm.1) | copy-start | bytes 11010052
  4.3 1.5 %copy-start.1 = (bf16[128,7168]{1,0:T(8,128)(2,1)S(1)}, bf16[128,7168]{1,0:T(8,128)(2,1)}, u32[]{:S(2)}) copy-start(bf16[128,7168]{1,0:T(8,128)(2,1)} %ow_hbm.1) | copy-start | bytes 5505028
  5.8 1.1 %copy-start.2 = (bf16[8,64,576]{2,1,0:T(8,128)(2,1)S(1)}, bf16[8,64,576]{2,1,0:T(8,128)(2,1)}, u32[]{:S(2)}) copy-start(bf16[8,64,576]{2,1,0:T(8,128)(2,1)} %cache_hbm.1) | copy-start | bytes 1769476
  6.9 1.1 %copy-start.3 = (bf16[448,576]{1,0:T(8,128)(2,1)S(1)}, bf16[448,576]{1,0:T(8,128)(2,1)}, u32[]{:S(2)}) copy-start(bf16[448,576]{1,0:T(8,128)(2,1)} %w_ref.1) | copy-start | bytes 1548292
  7.9 0.9 %copy-start.4 = (bf16[1,128,512]{2,1,0:T(8,128)(2,1)S(1)}, bf16[1,128,512]{2,1,0:T(8,128)(2,1)}, u32[]{:S(2)}) copy-start(bf16[1,128,512]{2,1,0:T(8,128)(2,1)} %param.22) | copy-start | bytes 393220
  8.8 0.9 %copy-start.5 = (bf16[1,512,128]{2,1,0:T(8,128)(2,1)S(1)}, bf16[1,512,128]{2,1,0:T(8,128)(2,1)}, u32[]{:S(2)}) copy-start(bf16[1,512,128]{2,1,0:T(8,128)(2,1)} %param.23) | copy-start | bytes 393220
  9.7 0.9 %copy-start.6 = (bf16[8,7168]{1,0:T(8,128)(2,1)S(1)}, bf16[8,7168]{1,0:T(8,128)(2,1)}, u32[]{:S(2)}) copy-start(bf16[8,7168]{1,0:T(8,128)(2,1)} %dh_ref.1) | copy-start | bytes 344068
  10.6 0.7 copy-start.7
  11.3 0.7 copy-start.8
  12.0 0.7 copy-start.9
  12.7 0.7 copy-start.10
  13.3 0.7 copy-start.11
  14.0 0.7 copy-start.12

commit v2 on v1

--- a/solution.py
+++ b/solution.py
@@ -122,12 +122,13 @@
 
 
 def fused_body(
-    plen, own, clen, w_ref, gain_ref, dh_ref, qn_ref, qr_ref, ka_ref, va_ref, tab_ref, dtab_ref,
+    plen_h, own_h, clen_h, w_h, gain_h, dh_h, qn_h, qr_h, ka_h, va_h,
     hid_hbm, ow_hbm, cache_hbm,
     new_ref, attn_ref,
-    wbuf, hb, ow, cb, acc, qbuf, kvs, kvr, msg, got, hp, rs, agp, ag, ent,
+    plen, own, clen, w_ref, gain_ref, dh_ref, qn_ref, qr_ref, ka_ref, va_ref, tab_ref,
+    wbuf, hb, ow, cb, acc, qbuf, kvs, kvr, msg, got, smsg, sgot, hp, rs, agp, ag, ent,
     loc, ring_s, core_s, x_s, in_r, core_r,
-    q_s, q_r, qc_s, qc_r, kv_s, kv_r, a_s, a_r, rs_s, rs_r, ag_s, ag_r, n_s, n_r,
+    q_s, q_r, qc_s, qc_r, kv_s, kv_r, a_s, a_r, s_s, s_r, rs_s, rs_r, ag_s, ag_r, n_s, n_r,
 ):
     me = lax.axis_index("heads")
     g = lax.axis_index("groups")
@@ -158,9 +159,16 @@
         pltpu.make_async_copy(hid_hbm, hb, loc.at[0]),
         pltpu.make_async_copy(ow_hbm, ow, loc.at[1]),
         pltpu.make_async_copy(cache_hbm, cb, loc.at[2]),
-        pltpu.make_async_copy(w_ref, wbuf.at[k, pl.ds(pl.multiple_of(c * rows, 16), rows)], loc.at[3]),
+        pltpu.make_async_copy(w_h, wbuf.at[k, pl.ds(pl.multiple_of(c * rows, 16), rows)], loc.at[3]),
     ]
-    for cp in (local_copies[3], local_copies[2], local_copies[0], local_copies[1]):
+    early = [
+        pltpu.make_async_copy(src, dst, loc.at[4 + n])
+        for n, (src, dst) in enumerate((
+            (ka_h, ka_ref), (qn_h, qn_ref), (qr_h, qr_ref), (dh_h, dh_ref), (w_h, w_ref), (clen_h, clen),
+            (gain_h, gain_ref), (va_h, va_ref), (plen_h, plen), (own_h, own),
+        ))
+    ]
+    for cp in early + [local_copies[2], local_copies[3], local_copies[1], local_copies[0]]:
         cp.start()
 
     barrier = pltpu.get_barrier_semaphore()
@@ -172,14 +180,14 @@
     lax.fori_loop(1, 16, greet, 0)
     pl.semaphore_signal(barrier, inc=1, device_id={"groups": 1 - g}, device_id_type=MESH)
 
-    starts = (304 * g, RING_A, 304 * (1 - g))
-    sizes = (RING_A, RING_C, RING_A)
+    starts = (304 * g, RING_A, 304 * (1 - g), 304 * (1 - g), 304 * (1 - g) + 80)
+    sizes = (RING_A, RING_C, RING_A, 80, 64)
 
     def piece(kk, cc, role):
         return wbuf.at[kk, pl.ds(pl.multiple_of(cc * rows + starts[role], 16), sizes[role])]
 
     def w_piece(role):
-        return w_ref.at[pl.ds(pl.multiple_of(starts[role], 16), sizes[role])]
+        return w_h.at[pl.ds(pl.multiple_of(starts[role], 16), sizes[role])]
 
     sends = []
 
@@ -200,6 +208,17 @@
             device_id=heads(dest), device_id_type=MESH,
         )
 
+    pl.semaphore_wait(barrier, 16)
+    for role in range(2):
+        mine = piece(k, c, role)
+        send(w_piece(role), mine, ring_s.at[0, k, role], in_r.at[k, role], heads(right))
+        send(w_piece(role), mine, ring_s.at[1, k, role], in_r.at[k, role], heads(left))
+    for role in range(3):
+        send(w_piece(role), piece(k, c, role), core_s.at[k, role], core_r.at[k, role], heads(sib))
+
+
+    for cp in early:
+        cp.wait()
     qlat = jnp.dot(qn_ref[...], ka_ref[...], preferred_element_type=f32).astype(bf16).astype(f32)
     q_own = jnp.concatenate([qlat, qr_ref[...].astype(f32)], axis=-1)
     qbuf[c, k] = q_own
@@ -207,8 +226,6 @@
     part = jnp.where(c == 0, wide[:, :rows], wide[:, rows:]).astype(bf16)
     kvs[0] = jnp.dot(part, w_ref[...], preferred_element_type=f32)
 
-    pl.semaphore_wait(barrier, 16)
-
     lax.fori_loop(1, 8, lambda i, t: (q_copy(i).start(), t)[1], 0)
 
     def kv_send(step):
@@ -221,13 +238,6 @@
         kvs[step + 1] = kvs[step] + kvr[step]
 
     kv_send(0)
-    for role in range(2):
-        mine = piece(k, c, role)
-        send(w_piece(role), mine, ring_s.at[0, k, role], in_r.at[k, role], heads(right))
-        send(w_piece(role), mine, ring_s.at[1, k, role], in_r.at[k, role], heads(left))
-    for role in range(3):
-        send(w_piece(role), piece(k, c, role), core_s.at[k, role], core_r.at[k, role], heads(sib))
-
     def to_core(kk, role):
         p = piece(kk, c, role)
         send(p, p, core_s.at[kk, role], core_r.at[kk, role], heads(sib))
@@ -241,17 +251,27 @@
             arrived(p, in_r.at[kk, role])
             if s < 3 or (s == 3 and role == way):
                 send(p, p, ring_s.at[way, kk, role], in_r.at[kk, role], heads(right if way == 0 else left))
-            if role == 0:
+            if role == 0 and s < 4:
                 send(p, p, x_s.at[kk], in_r.at[kk, 2], {"groups": 1 - g})
             to_core(kk, role)
 
     def cross(s):
-        for kk in (chip(pos - s), chip(pos + s)) if s < 4 else (chip(pos + 4),):
+        for way in range(2):
+            kk = chip(pos - s) if way == 0 else chip(pos + s)
             arrived(piece(kk, c, 2), in_r.at[kk, 2])
+            if s == 3:
+                p = piece(kk, c, 3 + way)
+                send(p, p, ring_s.at[way, kk, 2], in_r.at[kk, 3 + way], heads(right if way == 0 else left))
             to_core(kk, 2)
 
-    def matmul(kk, first=False):
-        for role in range(3):
+    def far():
+        kk = chip(pos + 4)
+        for role in (3, 4):
+            arrived(piece(kk, c, role), in_r.at[kk, role])
+            to_core(kk, role)
+
+    def matmul(kk, first=False, last=False):
+        for role in (0, 1, 3, 4) if last else (0, 1, 2):
             arrived(piece(kk, 1 - c, role), core_r.at[kk, role])
         h = hb[:, pl.ds(pl.multiple_of(kk * 2 * rows, 128), 2 * rows)]
         v = jnp.dot(h, wbuf[kk], preferred_element_type=f32)
@@ -268,6 +288,7 @@
 
     lax.fori_loop(1, 8, lambda i, t: (q_copy(i).wait_recv(), t)[1], 0)
     send(qbuf.at[c], qbuf.at[c], qc_s, qc_r, heads(sib))
+    ring(1, 0)
     kv_take(0)
     kv_send(1)
     local_copies[2].wait()
@@ -292,19 +313,38 @@
     pv = jnp.dot(wts.astype(bf16), cache[:, :lat], preferred_element_type=f32)
     lane = lax.broadcasted_iota(jnp.int32, (16 * n_req, 128), 1)
     stat = jnp.where(lane == 0, top, jnp.where(lane == 1, tot, 0.0))
-    msg[...] = jnp.concatenate([pv, stat], axis=-1).reshape(2, 8, n_req, lat + 128)
+    pv = pv.reshape(16, n_req, lat)
+    msg[...] = jnp.concatenate([pv[:, :, : lat // 2], pv[:, :, lat // 2 :]], axis=1).astype(bf16)
+    smsg[...] = stat.reshape(16, n_req, 128)
 
     def a_copy(i):
         dest = (me + i) % 16
         return pltpu.make_async_remote_copy(
-            src_ref=msg.at[dest % 2, dest // 2], dst_ref=got.at[me], send_sem=a_s.at[i], recv_sem=a_r.at[i],
+            src_ref=msg.at[(dest % 2) * 8 + dest // 2], dst_ref=got.at[me], send_sem=a_s.at[i], recv_sem=a_r.at[i],
             device_id=heads(dest), device_id_type=MESH,
         )
 
-    lax.fori_loop(1, 16, lambda i, t: (a_copy(i).start(), t)[1], 0)
-    got[me] = msg[c, k]
-
-    ring(1, 0)
+    def s_copy(i):
+        dest = (me + i) % 16
+        return pltpu.make_async_remote_copy(
+            src_ref=smsg.at[(dest % 2) * 8 + dest // 2], dst_ref=sgot.at[me], send_sem=s_s.at[i], recv_sem=s_r.at[i],
+            device_id=heads(dest), device_id_type=MESH,
+        )
+
+    lax.fori_loop(1, 16, lambda i, t: (a_copy(i).start(), s_copy(i).start(), t)[2], 0)
+    got[me] = msg[c * 8 + k]
+    sgot[me] = smsg[c * 8 + k]
+
+    slot = me // 8
+    m = hb.shape[0]
+    position = (me % 8) * m + lax.broadcasted_iota(jnp.int32, (m, 1), 0)
+    half = (width - lat) // 2
+    tab_ref[...] = rope_table(position, half)
+    req = lax.broadcasted_iota(jnp.int32, (n_req, 1), 0)
+    dpos = jnp.zeros((n_req, 1), jnp.int32)
+    for r in range(n_req):
+        dpos = jnp.where(req == r, clen[r], dpos)
+    dtab = rope_table(dpos, half)
     kv_take(1)
     kv_send(2)
     ring(1, 1)
@@ -312,48 +352,50 @@
     kv_send(3)
     ring(2, 0)
     kv_take(3)
-    own_key = finish(kvs[4], dtab_ref[...]).astype(bf16).astype(f32)
+    own_key = finish(kvs[4], dtab).astype(bf16).astype(f32)
     own_score = jnp.sum(q_own * own_key, axis=-1, keepdims=True) * scale
 
     def from_a(i, t):
         arrived(got.at[(me + 16 - i) % 16], a_r.at[i])
+        arrived(sgot.at[(me + 16 - i) % 16], s_r.at[i])
         return t
 
     lax.fori_loop(1, 16, from_a, 0)
-    gmax = got[:, :, lat : lat + 1]
-    gtot = got[:, :, lat + 1 : lat + 2]
+    gmax = sgot[:, :, 0:1]
+    gtot = sgot[:, :, 1:2]
     ceiling = jnp.maximum(jnp.max(gmax, axis=0), own_score)
     fac = jnp.exp(gmax - ceiling[None])
     own_w = jnp.exp(own_score - ceiling)
     summed = jnp.sum(fac * gtot, axis=0) + own_w
-    gath = jnp.sum(fac * got[:, :, :lat], axis=0) + own_w * own_key[:, :lat]
+    both = jnp.sum(jnp.concatenate([fac, fac], axis=1) * got[...].astype(f32), axis=0)
+    gath = jnp.concatenate([both[:n_req], both[n_req:]], axis=1) + own_w * own_key[:, :lat]
     lat_out = (gath / summed).astype(bf16)
     head_out = jnp.dot(lat_out, va_ref[...], preferred_element_type=f32).astype(bf16)
     local_copies[1].wait()
-    hp[...] = jnp.dot(head_out, ow[...], preferred_element_type=f32)
-
-    def span(d):
-        return pl.ds(pl.multiple_of((d // 2) * 896 + (d % 2) * 384, 128), 512)
+    flat = jnp.dot(head_out, ow[...], preferred_element_type=f32)
+    for d in range(16):
+        lo = (d // 2) * 896 + (d % 2) * 384
+        hp[d] = jnp.concatenate([flat[:, lo : lo + 256], flat[:, lo + 256 : lo + 512]], axis=0).astype(bf16)
 
     def rs_copy(i):
         dest = (me + i) % 16
         return pltpu.make_async_remote_copy(
-            src_ref=hp.at[:, span(dest)], dst_ref=rs.at[me], send_sem=rs_s.at[i], recv_sem=rs_r.at[i],
+            src_ref=hp.at[dest], dst_ref=rs.at[me], send_sem=rs_s.at[i], recv_sem=rs_r.at[i],
             device_id=heads(dest), device_id_type=MESH,
         )
 
     lax.fori_loop(1, 16, lambda i, t: (rs_copy(i).start(), t)[1], 0)
-    rs[me] = hp[:, span(me)]
+    rs[me] = hp[me]
     ring(2, 1)
     cross(1)
+    ring(3, 0)
 
     def from_rs(i, t):
         arrived(rs.at[(me + 16 - i) % 16], rs_r.at[i])
         return t
 
     lax.fori_loop(1, 16, from_rs, 0)
-    total = jnp.sum(rs[...], axis=0)
-    packed = jnp.concatenate([total[:, :256], total[:, 256:]], axis=0).astype(bf16)
+    packed = jnp.sum(rs[...].astype(f32), axis=0).astype(bf16)
     agp[...] = packed
     ag[me] = packed
 
@@ -365,7 +407,6 @@
         )
 
     lax.fori_loop(1, 16, lambda i, t: (ag_copy(i).start(), t)[1], 0)
-    ring(3, 0)
     cross(2)
     local_copies[0].wait()
     local_copies[3].wait()
@@ -388,17 +429,14 @@
         attn_ref[:, kk * 896 + 640 : kk * 896 + 896] = hi[8:].astype(bf16)
     matmul(chip(pos - 2))
     matmul(chip(pos + 2))
+    cross(3)
     ring(4, 0)
     ring(4, 1)
-    cross(3)
     matmul(chip(pos - 3))
     matmul(chip(pos + 3))
-    cross(4)
-    matmul(chip(pos + 4))
-
-    slot = me // 8
-    m = hb.shape[0]
-    position = (me % 8) * m + lax.broadcasted_iota(jnp.int32, (m, 1), 0)
+    far()
+    matmul(chip(pos + 4), last=True)
+
     e = jnp.where(position < plen[slot], finish(acc[...], tab_ref[...]), 0.0).astype(bf16)
     o_i = lax.broadcasted_iota(jnp.int32, (m, m), 0)
     s_i = lax.broadcasted_iota(jnp.int32, (m, m), 1)
@@ -424,6 +462,7 @@
 
     def drain(i, t):
         a_copy(i).wait_send()
+        s_copy(i).wait_send()
         rs_copy(i).wait_send()
         ag_copy(i).wait_send()
         return t
@@ -439,30 +478,29 @@
 
 
 def rope_table(positions, half):
-    frequency = jnp.exp(jnp.arange(half, dtype=jnp.float32) * (-math.log(10000.0) / half))
-    angles = positions.astype(jnp.float32)[:, None] * frequency
-    co, si = jnp.cos(angles), jnp.sin(angles)
-    return jnp.concatenate([co, co, -si, si], axis=-1)
+    lane = lax.broadcasted_iota(jnp.int32, (positions.shape[0], 4 * half), 1)
+    index = (lane % half).astype(jnp.float32)
+    angles = positions.astype(jnp.float32) * jnp.exp(index * (-math.log(10000.0) / half))
+    sine = jnp.where(lane < 3 * half, -jnp.sin(angles), jnp.sin(angles))
+    return jnp.where(lane < 2 * half, jnp.cos(angles), sine)
 
 
 def fused(
     prompt_hidden, prompt_len, owners, down_weight, latent_gain, decode_hidden, context_len,
     query_nope, query_rope, key_absorb, value_absorb, out_weight, cache,
 ):
-    device = lax.axis_index("heads")
     m, model = prompt_hidden.shape
     rows, width = down_weight.shape
     lat = latent_gain.shape[0]
-    half = (width - lat) // 2
     n_req = decode_hidden.shape[0]
     per_prompt = 16 // prompt_len.shape[0]
-    positions = (device % per_prompt) * m + jnp.arange(m, dtype=jnp.int32)
-    table = rope_table(positions, half)
-    dtable = rope_table(context_len, half)
     f32, bf16 = jnp.float32, jnp.bfloat16
+    small = (
+        prompt_len, owners, context_len, down_weight, latent_gain[None], decode_hidden, query_nope[:, 0],
+        query_rope[:, 0], key_absorb[0], value_absorb[0],
+    )
     vmem = pl.BlockSpec(memory_space=pltpu.VMEM)
-    smem = pl.BlockSpec(memory_space=pltpu.SMEM)
-    hbm = pl.BlockSpec(memory_space=pl.ANY)
+    hbm = pl.BlockSpec(memory_space=pltpu.HBM)
     dma = pltpu.SemaphoreType.DMA
     return pl.pallas_call(
         fused_body,
@@ -470,9 +508,12 @@
             jax.ShapeDtypeStruct((prompt_len.shape[0], m * per_prompt // 16, width), bf16),
             jax.ShapeDtypeStruct((n_req, model), bf16),
         ),
-        in_specs=[smem] * 3 + [vmem] * 9 + [hbm] * 3,
+        in_specs=[hbm] * (len(small) + 3),
         out_specs=(vmem, vmem),
-        scratch_shapes=[
+        scratch_shapes=[pltpu.SMEM(a.shape, a.dtype) for a in small[:3]]
+        + [pltpu.VMEM(a.shape, a.dtype) for a in small[3:]]
+        + [
+            pltpu.VMEM((m, 2 * (width - lat)), f32),
             pltpu.VMEM((8, 2 * rows, width), bf16),
             pltpu.VMEM((m, model), bf16),
             pltpu.VMEM(out_weight.shape, bf16),
@@ -481,32 +522,31 @@
             pltpu.VMEM((2, 8, n_req, width), f32),
             pltpu.VMEM((5, n_req, width), f32),
             pltpu.VMEM((4, n_req, width), f32),
-            pltpu.VMEM((2, 8, n_req, lat + 128), f32),
-            pltpu.VMEM((16, n_req, lat + 128), f32),
-            pltpu.VMEM((n_req, model), f32),
-            pltpu.VMEM((16, n_req, 512), f32),
+            pltpu.VMEM((16, 2 * n_req, lat // 2), bf16),
+            pltpu.VMEM((16, 2 * n_req, lat // 2), bf16),
+            pltpu.VMEM((16, n_req, 128), f32),
+            pltpu.VMEM((16, n_req, 128), f32),
+            pltpu.VMEM((16, 16, 256), bf16),
+            pltpu.VMEM((16, 16, 256), bf16),
             pltpu.VMEM((16, 256), bf16),
             pltpu.VMEM((16, 16, 256), bf16),
             pltpu.VMEM((16, m // 16, width), bf16),
-            dma((4,)),
-            dma((2, 8, 2)),
-            dma((8, 3)),
+            dma((16,)),
+            dma((2, 8, 3)),
+            dma((8, 5)),
             dma((8,)),
-            dma((8, 3)),
-            dma((8, 3)),
+            dma((8, 5)),
+            dma((8, 5)),
             dma((8,)), dma((8,)), dma, dma, dma((4,)), dma((4,)),
-            dma((16,)), dma((16,)), dma((16,)), dma((16,)), dma((16,)), dma((16,)), dma((16,)), dma((16,)),
+            dma((16,)), dma((16,)), dma((16,)), dma((16,)), dma((16,)), dma((16,)), dma((16,)), dma((16,)), dma((16,)), dma((16,)),
         ],
         compiler_params=pltpu.CompilerParams(
-            collective_id=0, has_side_effects=True, vmem_limit_bytes=44 * 1024 * 1024
+            collective_id=0, has_side_effects=True, vmem_limit_bytes=60 * 1024 * 1024
         ),
         cost_estimate=pl.CostEstimate(
             flops=2 * m * model * width, bytes_accessed=2 * (m * model + model * width), transcendentals=0
         ),
-    )(
-        prompt_len, owners, context_len, down_weight, latent_gain[None], decode_hidden, query_nope[:, 0],
-        query_rope[:, 0], key_absorb[0], value_absorb[0], table, dtable, prompt_hidden, out_weight, cache,
-    )
+    )(*small, prompt_hidden, out_weight, cache)
 
 
 def solution(mesh):

time: 90.4 us -> 75 us (0.83)
  local copies, waits for them, and re-layouts: 13.9 us -> 3.41 us
  Pallas kernels: 73.1 us -> 70.6 us
  other arithmetic: 1.57 us -> 0 us
    unnamed x27 -> x1, local copies, waits for them, and re-layouts: 13 us -> 1.55 us
    pallas_call x1, Pallas kernels: 73.1 us -> 70.6 us  [fused(): pl.pallas_call(fused_body, out_shape=(jax.ShapeDtypeStruct((prompt_len.sh...]
    pallas_call x1, local copies, waits for them, and re-layouts: 0.89 us -> 1.86 us  [fused(): pl.pallas_call(fused_body, out_shape=(jax.ShapeDtypeStruct((prompt_len.sh...]
where the time goes in v2:
time: 75 us; the launch traced here: 74.6 us
  Pallas kernels  70.6 us (94%)
  local copies, waits for them, and re-layouts  3.41 us (5%)
    pallas_call x1, Pallas kernels, fused(): pl.pallas_call(fused_body, out_shape=(jax.ShapeDtypeStruct((prompt_len.sh...  70.6 us
    pallas_call x1, local copies, waits for them, and re-layouts, fused(): pl.pallas_call(fused_body, out_shape=(jax.ShapeDtypeStruct((prompt_len.sh...  1.86 us
    unnamed x1, local copies, waits for them, and re-layouts  1.55 us

profile of v2, /device:TPU:1, one launch (start us, length us, event | category | flops | bytes accessed | tf_op | source)
XLA Modules:
  0.0 74.6 jit_solution(16194631304361073917)
XLA Ops:
  0.6 70.6 %shard_map.140 = (bf16[2,128,576]{2,1,0:T(8,128)(2,1)}, bf16[8,7168]{1,0:T(8,128)(2,1)}) custom-call(s32[2]{0:T(128)} %plen_h.1, s32[2]{0:T(128)} %own_h.1, s32[8]{0:T(128)} %clen_h.1, bf16[448,576]{1,0:T(8,128)(2,1)} %w_h.1, f32[1,512]{1,0:T(1,128)} %bitcast.7, bf16[8,7168]{1,0:T(8,128)(2,1)} %dh_h.1, bf16[8,128]{1,0:T(8,128)(2,1)} %bitcast.8, ...), custom_call_target="tpu_custom_call" | custom-call | flops 2113929216 | bytes 11927552 | tf_op jit(solution)/shard_map/pallas_call | solution.py:505
  71.2 1.9 %copy.15 = bf16[2,128,576]{1,2,0:T(8,128)(2,1)} copy(bf16[2,128,576]{2,1,0:T(8,128)(2,1)} %get-tuple-element.2) | data formatting | bytes 589824 | tf_op jit(solution)/shard_map/pallas_call | solution.py:505
  73.1 1.6 %copy.17 = bf16[8,7168]{1,0:T(8,128)(2,1)} copy(bf16[8,7168]{1,0:T(8,128)(2,1)} %get-tuple-element.7) | data formatting | bytes 229376

commit v3 on v2

--- a/solution.py
+++ b/solution.py
@@ -117,8 +117,10 @@
 
 
 MESH = pl.DeviceIdType.MESH
-RING_A = 144
-RING_C = 160
+RING_A = 176
+RING_C = 96
+RING = RING_A + RING_C
+FAR = 48
 
 
 def fused_body(
@@ -128,7 +130,7 @@
     plen, own, clen, w_ref, gain_ref, dh_ref, qn_ref, qr_ref, ka_ref, va_ref, tab_ref,
     wbuf, hb, ow, cb, acc, qbuf, kvs, kvr, msg, got, smsg, sgot, hp, rs, agp, ag, ent,
     loc, ring_s, core_s, x_s, in_r, core_r,
-    q_s, q_r, qc_s, qc_r, kv_s, kv_r, a_s, a_r, s_s, s_r, rs_s, rs_r, ag_s, ag_r, n_s, n_r,
+    q_s, q_r, qc_s, qc_r, agc_s, agc_r, kv_s, kv_r, a_s, a_r, s_s, s_r, rs_s, rs_r, ag_s, ag_r, n_s, n_r,
 ):
     me = lax.axis_index("heads")
     g = lax.axis_index("groups")
@@ -180,8 +182,8 @@
     lax.fori_loop(1, 16, greet, 0)
     pl.semaphore_signal(barrier, inc=1, device_id={"groups": 1 - g}, device_id_type=MESH)
 
-    starts = (304 * g, RING_A, 304 * (1 - g), 304 * (1 - g), 304 * (1 - g) + 80)
-    sizes = (RING_A, RING_C, RING_A, 80, 64)
+    starts = (RING * g, RING_A, RING * (1 - g), RING * (1 - g), RING * (1 - g) + FAR)
+    sizes = (RING_A, RING_C, RING_A, FAR, RING_A - FAR)
 
     def piece(kk, cc, role):
         return wbuf.at[kk, pl.ds(pl.multiple_of(cc * rows + starts[role], 16), sizes[role])]
@@ -221,7 +223,9 @@
         cp.wait()
     qlat = jnp.dot(qn_ref[...], ka_ref[...], preferred_element_type=f32).astype(bf16).astype(f32)
     q_own = jnp.concatenate([qlat, qr_ref[...].astype(f32)], axis=-1)
-    qbuf[c, k] = q_own
+    fold = 384
+    tail = jnp.concatenate([q_own[:, fold:], jnp.zeros((q_own.shape[0], 2 * fold - width), f32)], axis=-1)
+    qbuf[c, k] = jnp.concatenate([q_own[:, :fold], tail], axis=0).astype(bf16)
     wide = dh_ref[:, pl.ds(pl.multiple_of(k * 2 * rows, 128), 2 * rows)].astype(f32)
     part = jnp.where(c == 0, wide[:, :rows], wide[:, rows:]).astype(bf16)
     kvs[0] = jnp.dot(part, w_ref[...], preferred_element_type=f32)
@@ -297,7 +301,14 @@
     n_req = cb.shape[0]
     per = cb.shape[1]
     cols = n_req * per
-    q_all = qbuf[...].reshape(16 * n_req, width).astype(bf16)
+    q_all = qbuf[...].astype(f32).reshape(16, 2 * n_req, fold)
+    q_all = jnp.concatenate(
+        [
+            q_all[:, :n_req].reshape(16 * n_req, fold),
+            q_all[:, n_req:].reshape(16 * n_req, fold)[:, : width - fold],
+        ],
+        axis=-1,
+    ).astype(bf16)
     cache = cb[...].reshape(cols, width)
     scores = lax.dot_general(q_all, cache, (((1,), (1,)), ((), ())), preferred_element_type=f32) * scale
     row_i = lax.broadcasted_iota(jnp.int32, scores.shape, 0)
@@ -397,39 +408,41 @@
     lax.fori_loop(1, 16, from_rs, 0)
     packed = jnp.sum(rs[...].astype(f32), axis=0).astype(bf16)
     agp[...] = packed
-    ag[me] = packed
+    ag[c, k] = packed
 
     def ag_copy(i):
-        dest = (me + i) % 16
+        dest = ((k + i) % 8) * 2 + c
         return pltpu.make_async_remote_copy(
-            src_ref=agp, dst_ref=ag.at[me], send_sem=ag_s.at[i], recv_sem=ag_r.at[i],
+            src_ref=agp, dst_ref=ag.at[c, k], send_sem=ag_s.at[i], recv_sem=ag_r.at[i],
             device_id=heads(dest), device_id_type=MESH,
         )
 
-    lax.fori_loop(1, 16, lambda i, t: (ag_copy(i).start(), t)[1], 0)
+    lax.fori_loop(1, 8, lambda i, t: (ag_copy(i).start(), t)[1], 0)
     cross(2)
     local_copies[0].wait()
     local_copies[3].wait()
     matmul(k, True)
     ring(3, 1)
+    cross(3)
     matmul(chip(pos - 1))
     matmul(chip(pos + 1))
 
     def from_ag(i, t):
-        arrived(ag.at[(me + 16 - i) % 16], ag_r.at[i])
+        arrived(ag.at[c, (k + 8 - i) % 8], ag_r.at[i])
         return t
 
-    lax.fori_loop(1, 16, from_ag, 0)
+    lax.fori_loop(1, 8, from_ag, 0)
+    send(ag.at[c], ag.at[c], agc_s, agc_r, heads(sib))
+    matmul(chip(pos - 2))
+    matmul(chip(pos + 2))
+    arrived(ag.at[1 - c], agc_r)
     for kk in range(8):
-        lo = ag[2 * kk].astype(f32)
-        hi = ag[2 * kk + 1].astype(f32)
+        lo = ag[0, kk].astype(f32)
+        hi = ag[1, kk].astype(f32)
         attn_ref[:, kk * 896 : kk * 896 + 256] = lo[:8].astype(bf16)
         attn_ref[:, kk * 896 + 256 : kk * 896 + 512] = lo[8:].astype(bf16)
         attn_ref[:, kk * 896 + 512 : kk * 896 + 640] = hi[:8, 128:].astype(bf16)
         attn_ref[:, kk * 896 + 640 : kk * 896 + 896] = hi[8:].astype(bf16)
-    matmul(chip(pos - 2))
-    matmul(chip(pos + 2))
-    cross(3)
     ring(4, 0)
     ring(4, 1)
     matmul(chip(pos - 3))
@@ -458,13 +471,12 @@
     new_ref[slot, pl.ds(pl.multiple_of((me % 8) * 16, 16), 16)] = ent[me]
     for cp in sends:
         cp.wait_send()
-    lax.fori_loop(1, 8, lambda i, t: (q_copy(i).wait_send(), t)[1], 0)
+    lax.fori_loop(1, 8, lambda i, t: (q_copy(i).wait_send(), ag_copy(i).wait_send(), t)[2], 0)
 
     def drain(i, t):
         a_copy(i).wait_send()
         s_copy(i).wait_send()
         rs_copy(i).wait_send()
-        ag_copy(i).wait_send()
         return t
 
     lax.fori_loop(1, 16, drain, 0)
@@ -519,7 +531,7 @@
             pltpu.VMEM(out_weight.shape, bf16),
             pltpu.VMEM(cache.shape, bf16),
             pltpu.VMEM((m, width), f32),
-            pltpu.VMEM((2, 8, n_req, width), f32),
+            pltpu.VMEM((2, 8, 2 * n_req, 384), bf16),
             pltpu.VMEM((5, n_req, width), f32),
             pltpu.VMEM((4, n_req, width), f32),
             pltpu.VMEM((16, 2 * n_req, lat // 2), bf16),
@@ -529,7 +541,7 @@
             pltpu.VMEM((16, 16, 256), bf16),
             pltpu.VMEM((16, 16, 256), bf16),
             pltpu.VMEM((16, 256), bf16),
-            pltpu.VMEM((16, 16, 256), bf16),
+            pltpu.VMEM((2, 8, 16, 256), bf16),
             pltpu.VMEM((16, m // 16, width), bf16),
             dma((16,)),
             dma((2, 8, 3)),
@@ -537,7 +549,7 @@
             dma((8,)),
             dma((8, 5)),
             dma((8, 5)),
-            dma((8,)), dma((8,)), dma, dma, dma((4,)), dma((4,)),
+            dma((8,)), dma((8,)), dma, dma, dma, dma, dma((4,)), dma((4,)),
             dma((16,)), dma((16,)), dma((16,)), dma((16,)), dma((16,)), dma((16,)), dma((16,)), dma((16,)), dma((16,)), dma((16,)),
         ],
         compiler_params=pltpu.CompilerParams(

time: 75 us -> 70.2 us (0.936)
  Pallas kernels: 70.6 us -> 66 us
    pallas_call x1, Pallas kernels: 70.6 us -> 66 us  [fused(): pl.pallas_call(fused_body, out_shape=(jax.ShapeDtypeStruct((prompt_len.sh...]
where the time goes in v3:
time: 70.2 us; the launch traced here: 70.1 us
  Pallas kernels  66 us (94%)
  local copies, waits for them, and re-layouts  3.41 us (5%)
    pallas_call x1, Pallas kernels, fused(): pl.pallas_call(fused_body, out_shape=(jax.ShapeDtypeStruct((prompt_len.sh...  66 us
    pallas_call x1, local copies, waits for them, and re-layouts, fused(): pl.pallas_call(fused_body, out_shape=(jax.ShapeDtypeStruct((prompt_len.sh...  1.86 us
    unnamed x1, local copies, waits for them, and re-layouts  1.55 us

profile of v3, /device:TPU:1, one launch (start us, length us, event | category | flops | bytes accessed | tf_op | source)
XLA Modules:
  0.0 70.1 jit_solution(2399379322512193509)
XLA Ops:
  0.6 66.0 %shard_map.140 = (bf16[2,128,576]{2,1,0:T(8,128)(2,1)}, bf16[8,7168]{1,0:T(8,128)(2,1)}) custom-call(s32[2]{0:T(128)} %plen_h.1, s32[2]{0:T(128)} %own_h.1, s32[8]{0:T(128)} %clen_h.1, bf16[448,576]{1,0:T(8,128)(2,1)} %w_h.1, f32[1,512]{1,0:T(1,128)} %bitcast.7, bf16[8,7168]{1,0:T(8,128)(2,1)} %dh_h.1, bf16[8,128]{1,0:T(8,128)(2,1)} %bitcast.8, ...), custom_call_target="tpu_custom_call" | custom-call | flops 2113929216 | bytes 11927552 | tf_op jit(solution)/shard_map/pallas_call | solution.py:517
  66.7 1.9 %copy.15 = bf16[2,128,576]{1,2,0:T(8,128)(2,1)} copy(bf16[2,128,576]{2,1,0:T(8,128)(2,1)} %get-tuple-element.2) | data formatting | bytes 589824 | tf_op jit(solution)/shard_map/pallas_call | solution.py:517
  68.5 1.6 %copy.17 = bf16[8,7168]{1,0:T(8,128)(2,1)} copy(bf16[8,7168]{1,0:T(8,128)(2,1)} %get-tuple-element.7) | data formatting | bytes 229376

commit v4 on v3

--- a/solution.py
+++ b/solution.py
@@ -128,7 +128,7 @@
     hid_hbm, ow_hbm, cache_hbm,
     new_ref, attn_ref,
     plen, own, clen, w_ref, gain_ref, dh_ref, qn_ref, qr_ref, ka_ref, va_ref, tab_ref,
-    wbuf, hb, ow, cb, acc, qbuf, kvs, kvr, msg, got, smsg, sgot, hp, rs, agp, ag, ent,
+    wbuf, hb, ow, cb, acc, qbuf, kvs, kvr, msg, got, smsg, sgot, hp, rs, agp, ag, ent, perm_ref,
     loc, ring_s, core_s, x_s, in_r, core_r,
     q_s, q_r, qc_s, qc_r, agc_s, agc_r, kv_s, kv_r, a_s, a_r, s_s, s_r, rs_s, rs_r, ag_s, ag_r, n_s, n_r,
 ):
@@ -447,15 +447,15 @@
     ring(4, 1)
     matmul(chip(pos - 3))
     matmul(chip(pos + 3))
-    far()
-    matmul(chip(pos + 4), last=True)
-
-    e = jnp.where(position < plen[slot], finish(acc[...], tab_ref[...]), 0.0).astype(bf16)
     o_i = lax.broadcasted_iota(jnp.int32, (m, m), 0)
     s_i = lax.broadcasted_iota(jnp.int32, (m, m), 1)
     turn = (o_i // 16 - own[slot] + 16) % 16
-    perm = jnp.where(s_i == (o_i % 16) * 16 + turn, 1.0, 0.0).astype(bf16)
-    ent[...] = jnp.dot(perm, e, preferred_element_type=f32).astype(bf16).reshape(ent.shape)
+    perm_ref[...] = jnp.where(s_i == (o_i % 16) * 16 + turn, 1.0, 0.0).astype(bf16)
+    far()
+    matmul(chip(pos + 4), last=True)
+
+    e = jnp.where(position < plen[slot], finish(acc[...], tab_ref[...]), 0.0).astype(bf16)
+    ent[...] = jnp.dot(perm_ref[...], e, preferred_element_type=f32).astype(bf16).reshape(ent.shape)
 
     def dst_of(src):
         return new_ref.at[src // 8, pl.ds(pl.multiple_of((src % 8) * 16, 16), 16)]
@@ -543,6 +543,7 @@
             pltpu.VMEM((16, 256), bf16),
             pltpu.VMEM((2, 8, 16, 256), bf16),
             pltpu.VMEM((16, m // 16, width), bf16),
+            pltpu.VMEM((m, m), bf16),
             dma((16,)),
             dma((2, 8, 3)),
             dma((8, 5)),

time: 70.2 us -> 70.2 us (level)
  no operation moved by 1% of the time
where the time goes in v4:
time: 70.2 us; the launch traced here: 70 us
  Pallas kernels  65.9 us (94%)
  local copies, waits for them, and re-layouts  3.41 us (5%)
    pallas_call x1, Pallas kernels, fused(): pl.pallas_call(fused_body, out_shape=(jax.ShapeDtypeStruct((prompt_len.sh...  65.9 us
    pallas_call x1, local copies, waits for them, and re-layouts, fused(): pl.pallas_call(fused_body, out_shape=(jax.ShapeDtypeStruct((prompt_len.sh...  1.86 us
    unnamed x1, local copies, waits for them, and re-layouts  1.55 us

profile of v4, /device:TPU:1, one launch (start us, length us, event | category | flops | bytes accessed | tf_op | source)
XLA Modules:
  0.0 70.0 jit_solution(1025576294883948315)
XLA Ops:
  0.6 65.9 %shard_map.140 = (bf16[2,128,576]{2,1,0:T(8,128)(2,1)}, bf16[8,7168]{1,0:T(8,128)(2,1)}) custom-call(s32[2]{0:T(128)} %plen_h.1, s32[2]{0:T(128)} %own_h.1, s32[8]{0:T(128)} %clen_h.1, bf16[448,576]{1,0:T(8,128)(2,1)} %w_h.1, f32[1,512]{1,0:T(1,128)} %bitcast.7, bf16[8,7168]{1,0:T(8,128)(2,1)} %dh_h.1, bf16[8,128]{1,0:T(8,128)(2,1)} %bitcast.8, ...), custom_call_target="tpu_custom_call" | custom-call | flops 2113929216 | bytes 11927552 | tf_op jit(solution)/shard_map/pallas_call | solution.py:517
  66.6 1.9 %copy.15 = bf16[2,128,576]{1,2,0:T(8,128)(2,1)} copy(bf16[2,128,576]{2,1,0:T(8,128)(2,1)} %get-tuple-element.2) | data formatting | bytes 589824 | tf_op jit(solution)/shard_map/pallas_call | solution.py:517
  68.4 1.6 %copy.17 = bf16[8,7168]{1,0:T(8,128)(2,1)} copy(bf16[8,7168]{1,0:T(8,128)(2,1)} %get-tuple-element.7) | data formatting | bytes 229376
